TPU v7x, 512 devices: a whole 4x8x8 slice. The times are simulated.
512 devices in a mesh: section: 4 (over x), elem: 128 (over y, z, core).
Axes of the slice: x: 4, y: 8, z: 8, core: 2. Of those that a mesh axis runs over, the one named last changes fastest.
Arguments:
- section_residual: float32 [4, 5, 64, 16384], P('section', None, None, 'elem'), may hold values from -110 to 110
- transform: float32 [4, 4], replicated, may hold values from -0.9 to 3.9
- shifts: float32 [4], P('section'), may hold values from 1 to 4
- linear_flux_matrix: float32 [3, 5, 5, 16384], P(None, None, None, 'elem'), may hold values from -1 to 1
- penalty: float32 [6, 16384], P(None, 'elem'), may hold values from 0.2 to 1
- block_inverse_factor: float32 [4, 5, 5, 16384], P('section', None, None, 'elem'), may hold values from -2.5 to 2.5
- nodal_inverse_factor: float32 [4, 64, 64], P('section'), may hold values from -0.75 to 0.75
- neighbours: int32 [6, 16384], P(None, 'elem'), may hold values from -1 to 16383, as said below
- orientation: int32 [6, 16384], P(None, 'elem'), may hold values from 0 to 7
- live_counts: int32 [128], P('elem'), may hold values from 112 to 128, as said below
Outputs:
- section_update: float32 [4, 5, 64, 16384], P('section', None, None, 'elem')
- start_rms: float32 [4], P('section')
Inputs may be any that keep to these rules, and one draw needn't show every extreme that they name: `neighbours`: row f names for face f of element slot g = d * 128 + l the global slot of the element across it, or -1 at walls, at the ends of the slab and for every face of a slot that is not live. Every named slot is live. An element named on another device lies on device d - 1 within its last 32 slots or on device d + 1 within its first 32 slots. Faces f and f xor 1 are opposite, and the relation is symmetric. `live_counts`: live slots of a device come first; the last device is full.
All inputs are finite; a program needn't handle non-finite values.
Results may differ from a plain program's by a relative error of at most 0.0003.
Values sent between devices are 32-bit elements; how exact they have to be, the bound alone decides.
A program may use at most 64 MiB of HBM per device.

v0:
```python
import jax
import jax.numpy as jnp
import numpy as np
from jax import lax
from jax.sharding import PartitionSpec as P

TOP_PRECISION = lax.Precision.HIGHEST


def padded(block, sides, width):
    for axis, dim in sides:
        count = lax.axis_size(axis)
        forward = [(i, i + 1) for i in range(count - 1)]
        backward = [(target, source) for source, target in forward]
        low = lax.ppermute(
            lax.slice_in_dim(block, block.shape[dim] - width, None, axis=dim), axis, forward
        )
        high = lax.ppermute(lax.slice_in_dim(block, 0, width, axis=dim), axis, backward)
        block = jnp.concatenate([low, block, high], axis=dim)
    return block


def derivative_table():
    points = np.array([-1.0, -np.sqrt(0.2), np.sqrt(0.2), 1.0])
    weights = np.array(
        [
            1.0
            / np.prod(
                [
                    points[column] - points[other_point]
                    for other_point in range(4)
                    if other_point != column
                ]
            )
            for column in range(4)
        ]
    )
    table = np.zeros((4, 4))
    for row_at in range(4):
        for column in range(4):
            if row_at != column:
                table[row_at, column] = (
                    weights[column] / weights[row_at] / (points[row_at] - points[column])
                )
        table[row_at, row_at] = -np.sum(table[row_at])
    return table


def partner_table():
    corner = np.arange(64).reshape(4, 4, 4)
    face_list = [corner[0], corner[3], corner[:, 0], corner[:, 3], corner[:, :, 0], corner[:, :, 3]]
    partner = np.zeros((6, 8, 16), np.int32)
    for face_id in range(6):
        opposite = face_list[face_id ^ 1]
        for code_id in range(8):
            for place_one in range(4):
                for place_two in range(4):
                    index_one, index_two = (place_one, place_two)
                    if code_id & 4:
                        index_one, index_two = (index_two, index_one)
                    if code_id & 1:
                        index_one = 3 - index_one
                    if code_id & 2:
                        index_two = 3 - index_two
                    partner[face_id, code_id, place_one * 4 + place_two] = opposite[
                        index_one, index_two
                    ]
    return partner


def face_selectors():
    full = slice(None)
    return [
        (full, 0),
        (full, 3),
        (full, full, 0),
        (full, full, 3),
        (full, full, full, 0),
        (full, full, full, 3),
    ]


def partner_nodes(orientation):
    code_list = jnp.arange(8, dtype=jnp.int32)
    matches = orientation[:, None, None, :] == code_list[None, :, None, None]
    table = jnp.asarray(partner_table(), dtype=jnp.int32)
    return jnp.sum(jnp.where(matches, table[:, :, :, None], 0), axis=1)


def invert_small(matrix):
    order_of = matrix.shape[0]
    left_part = matrix
    right_part = jnp.eye(order_of, dtype=matrix.dtype)
    for pivot_at in range(order_of):
        pivot_scale = 1.0 / left_part[pivot_at, pivot_at]
        left_part = left_part.at[pivot_at].multiply(pivot_scale)
        right_part = right_part.at[pivot_at].multiply(pivot_scale)
        for target in range(order_of):
            if target != pivot_at:
                factor = left_part[target, pivot_at]
                left_part = left_part.at[target].add(-factor * left_part[pivot_at])
                right_part = right_part.at[target].add(-factor * right_part[pivot_at])
    return right_part


def operate(
    source_term,
    extended,
    shift_value,
    linear_flux_matrix,
    penalty,
    far_slots,
    has_partner,
    node_index,
    active_mask,
):
    derivative = jnp.asarray(derivative_table(), dtype=source_term.dtype)
    element_count = source_term.shape[2]
    padded_width = extended.shape[2]
    cube_view = source_term.reshape(5, 4, 4, 4, element_count)
    section_slopes = [
        jnp.einsum("ai,vijke->vajke", derivative, cube_view, precision=TOP_PRECISION),
        jnp.einsum("aj,vijke->viake", derivative, cube_view, precision=TOP_PRECISION),
        jnp.einsum("ak,vijke->vijae", derivative, cube_view, precision=TOP_PRECISION),
    ]
    computed_output = shift_value * source_term
    for axis_direction in range(3):
        computed_output = computed_output + jnp.einsum(
            "kch,cfh->kfh",
            linear_flux_matrix[axis_direction],
            section_slopes[axis_direction].reshape(5, 64, element_count),
            precision=TOP_PRECISION,
        )
    flat_index = (node_index * padded_width + far_slots[:, None, :]).reshape(96 * element_count)
    far_trace = jnp.take(extended.reshape(5, 64 * padded_width), flat_index, axis=1).reshape(
        5, 6, 16, element_count
    )
    far_trace = far_trace * has_partner[None, :, None, :]
    result_cube = computed_output.reshape(5, 4, 4, 4, element_count)
    for face_id, selector in enumerate(face_selectors()):
        own_trace = cube_view[selector]
        face_jump = (own_trace - far_trace[:, face_id].reshape(5, 4, 4, element_count)) * penalty[
            face_id
        ]
        result_cube = result_cube.at[selector].add(face_jump)
    return result_cube.reshape(5, 64, element_count) * active_mask


def precondition(source_term, block_inverse_factor, nodal_inverse_factor, active_mask):
    spread_output = jnp.einsum(
        "ab,cbx->cax", nodal_inverse_factor, source_term, precision=TOP_PRECISION
    )
    return (
        jnp.einsum("kch,cfh->kfh", block_inverse_factor, spread_output, precision=TOP_PRECISION)
        * active_mask
    )


def small_solve(start_norm, column_one, column_two):
    top_norm = jnp.sqrt(jnp.sum(column_one * column_one))
    unit_one = column_one / top_norm
    cross_term = jnp.sum(unit_one * column_two)
    remainder = column_two - cross_term * unit_one
    rest_norm = jnp.sqrt(jnp.sum(remainder * remainder))
    coef_two = start_norm * remainder[0] / (rest_norm * rest_norm)
    coef_one = (start_norm * unit_one[0] - cross_term * coef_two) / top_norm
    return (coef_one, coef_two)


def project_one(mapped, vector):
    return lax.psum(jnp.sum(mapped * vector), "elem")


def orth_length(mapped):
    return jnp.sqrt(lax.psum(jnp.sum(mapped * mapped), "elem"))


def orthogonalize(mapped, krylov_basis):
    coefficients = []
    for vector in krylov_basis:
        coefficient = project_one(mapped, vector)
        mapped = mapped - coefficient * vector
        coefficients.append(coefficient)
    length = orth_length(mapped)
    return (coefficients, length, mapped)


def extend_source(source_term, band_width):
    extended = padded(source_term, (("elem", 2),), band_width)
    return extended


def local(
    section_residual,
    transform,
    shifts,
    linear_flux_matrix,
    penalty,
    block_inverse_factor,
    nodal_inverse_factor,
    neighbours,
    orientation,
    live_counts,
):
    element_count = section_residual.shape[3]
    band_width = element_count // 4
    section_id = lax.axis_index("section")
    device = lax.axis_index("elem")
    active_mask = (jnp.arange(element_count, dtype=jnp.int32) < live_counts[0]).astype(jnp.float32)
    inverse = invert_small(transform)
    every_section = lax.all_gather(section_residual, "section", axis=0, tiled=True)
    own_row = lax.dynamic_slice_in_dim(inverse, section_id, 1, 0)
    mixed_rhs = jnp.einsum("st,tvne->svne", own_row, every_section, precision=TOP_PRECISION)
    right_side = mixed_rhs[0] * active_mask
    has_partner = (neighbours >= 0).astype(jnp.float32)
    far_slots = jnp.where(neighbours >= 0, neighbours - device * element_count + band_width, 0)
    node_index = partner_nodes(orientation)
    shift_value = shifts[0]
    start_norm = jnp.sqrt(lax.psum(jnp.sum(right_side * right_side), "elem"))
    entry_total = 5 * 64 * element_count * lax.axis_size("elem")
    start_rms = (start_norm / jnp.sqrt(jnp.asarray(entry_total, dtype=jnp.float32)))[None]
    krylov_basis = [right_side / start_norm]
    directions = []
    columns = []
    for column in range(2):
        axis_direction = precondition(
            krylov_basis[column], block_inverse_factor[0], nodal_inverse_factor[0], active_mask
        )
        directions.append(axis_direction)
        extended = extend_source(axis_direction, band_width)
        mapped = operate(
            axis_direction,
            extended,
            shift_value,
            linear_flux_matrix,
            penalty,
            far_slots,
            has_partner,
            node_index,
            active_mask,
        )
        coefficients, length, mapped = orthogonalize(mapped, krylov_basis)
        krylov_basis.append(mapped / length)
        columns.append(coefficients + [length])
    column_one = jnp.stack(columns[0] + [jnp.zeros_like(start_norm)])
    column_two = jnp.stack(columns[1])
    coef_one, coef_two = small_solve(start_norm, column_one, column_two)
    solution = (coef_one * directions[0] + coef_two * directions[1])[None]
    every_solution = lax.all_gather(solution, "section", axis=0, tiled=True)
    own_row = lax.dynamic_slice_in_dim(transform, section_id, 1, 0)
    section_update = jnp.einsum("st,tvne->svne", own_row, every_solution, precision=TOP_PRECISION)
    return (section_update, start_rms)


def solution(mesh):
    placed = (
        P("section", None, None, "elem"),
        P(),
        P("section"),
        P(None, None, None, "elem"),
        P(None, "elem"),
        P("section", None, None, "elem"),
        P("section", None, None),
        P(None, "elem"),
        P(None, "elem"),
        P("elem"),
    )
    return jax.shard_map(
        local,
        mesh=mesh,
        in_specs=placed,
        out_specs=(P("section", None, None, "elem"), P("section")),
        check_vma=False,
    )
```

profile of v0, /device:TPU:1, one launch (start us, length us, event | category | flops | bytes accessed | tf_op | source)
XLA Modules:
  0.0 1740.7 jit_solution(16648848644469391593)
XLA Ops:
  0.7 1.2 slice.1128
  22.7 11.5 all_gather.6
  34.9 1.5 fusion.2
  37.1 257.3 %psum.42 = f32[]{:T(128)} all-reduce(f32[]{:T(128)} %multiply_reduce_fusion.5), channel_id=1, replica_groups=mesh['section'=4,'elem'=128] {'elem'}, use_global_device_ids=true, to_apply=%region_1.0 | all-reduce | flops 1 | bytes 8 | tf_op jit(solution)/shard_map/psum | solution.py:219
  296.6 1.0 fusion.6
  298.6 1.9 collective-permute-start
  300.5 5.5 collective-permute-start.1
  308.9 1.0 fusion.18
  311.2 1.0 fusion.14
  314.3 1.8 fusion.10
  316.1 1.2 copy.193
  317.9 1.0 bitcast_add_fusion.3
  319.9 1.2 pad_maximum_fusion
  321.1 4.2 copy.230
  325.3 43.8 %gather_fusion = f32[12288,5]{1,0:T(8,128)} fusion(f32[5,12288]{0,1:T(8,128)} %bitcast.216, s32[12288]{0:T(1024)S(1)} %fusion.60), kind=kCustom, calls=%fused_computation.clone | custom fusion | bytes 540672 | tf_op jit(solution)/shard_map/jit(_take)/gather | solution.py:135
  369.1 10.3 broadcast_select_fusion.1
  379.4 4.4 copy.195
  384.2 1.5 scatter-add.136
  385.8 1.5 scatter-add.139
  388.1 246.2 %psum.43 = f32[]{:T(128)} all-reduce(f32[]{:T(128)} %multiply_reduce_fusion.4), channel_id=1, replica_groups=mesh['section'=4,'elem'=128] {'elem'}, use_global_device_ids=true, to_apply=%region_4.6 | all-reduce | flops 1 | bytes 8 | tf_op jit(solution)/shard_map/psum | solution.py:171
  634.3 1.3 multiply_reduce_fusion.3
  635.6 248.8 %psum.44 = f32[]{:T(128)} all-reduce(f32[]{:T(128)} %multiply_reduce_fusion.3), channel_id=1, replica_groups=mesh['section'=4,'elem'=128] {'elem'}, use_global_device_ids=true, to_apply=%region_6.8 | all-reduce | flops 1 | bytes 8 | tf_op jit(solution)/shard_map/psum | solution.py:175
  886.3 1.8 fusion.4
  888.1 1.2 copy.204
  891.3 1.9 collective-permute-start.2
  893.3 3.0 collective-permute-start.3
  897.0 1.1 copy.207
  898.2 1.8 fusion.16
  900.0 1.9 copy.208
  902.1 1.0 fusion.12
  903.5 1.0 fusion.8
  905.7 1.2 pad_maximum_fusion.1
  906.8 4.2 copy.231
  911.0 43.8 %gather_fusion.1 = f32[12288,5]{1,0:T(8,128)} fusion(f32[5,12288]{0,1:T(8,128)} %bitcast.215, s32[12288]{0:T(1024)S(1)} %fusion.60), kind=kCustom, calls=%fused_computation.1.clone | custom fusion | bytes 540672 | tf_op jit(solution)/shard_map/jit(_take)/gather | solution.py:135
  954.9 10.3 broadcast_select_fusion
  965.2 4.4 copy.216
  970.0 1.5 scatter-add.146
  971.6 1.5 scatter-add.149
  973.8 246.2 %psum.45 = f32[]{:T(128)} all-reduce(f32[]{:T(128)} %multiply_reduce_fusion.2), channel_id=1, replica_groups=mesh['section'=4,'elem'=128] {'elem'}, use_global_device_ids=true, to_apply=%region_9.11 | all-reduce | flops 1 | bytes 8 | tf_op jit(solution)/shard_map/psum | solution.py:171
  1220.1 1.4 multiply_reduce_fusion.1
  1221.5 1.3 multiply_reduce_fusion.8
  1222.8 248.4 %psum.46 = f32[]{:T(128)} all-reduce(f32[]{:T(128)} %multiply_reduce_fusion.1), channel_id=1, replica_groups=mesh['section'=4,'elem'=128] {'elem'}, use_global_device_ids=true, to_apply=%region_11.13 | all-reduce | flops 1 | bytes 8 | tf_op jit(solution)/shard_map/psum | solution.py:171
  1471.2 2.0 multiply_reduce_fusion
  1473.8 247.3 %psum.47 = f32[]{:T(128)} all-reduce(f32[]{:T(128)} %multiply_reduce_fusion), channel_id=1, replica_groups=mesh['section'=4,'elem'=128] {'elem'}, use_global_device_ids=true, to_apply=%region_13.15 | all-reduce | flops 1 | bytes 8 | tf_op jit(solution)/shard_map/psum | solution.py:175
  1721.9 1.9 multiply_reduce_fusion.7
  1723.8 1.2 multiply_reduce_fusion.6
  1726.6 10.2 all-gather
  1736.7 2.9 fusion
  (166 shorter events, 28.2 us)
Async XLA Ops:
  0.6 294.5 %copy-start = (f32[1,64,64]{2,1,0:T(8,128)S(1)}, f32[1,64,64]{2,1,0:T(8,128)}, u32[]{:S(2)}) copy-start(f32[1,64,64]{2,1,0:T(8,128)} %param.107) | copy-start | bytes 49156
  0.6 305.5 %copy-start.3 = (s32[6,8,16]{2,1,0:T(8,128)S(1)}, s32[6,8,16]{2,1,0:T(8,128)}, u32[]{:S(2)}) copy-start(s32[6,8,16]{2,1,0:T(8,128)} %constant.971.clone) | copy-start | bytes 9220
  0.7 305.7 %copy-start.1 = (f32[4,4,1,1,1]{1,0,4,3,2:T(4,128)S(1)}, f32[4,4,1,1,1]{1,0,4,3,2:T(4,128)}, u32[]{:S(2)}) copy-start(f32[4,4,1,1,1]{1,0,4,3,2:T(4,128)} %constant.978) | copy-start | bytes 196
  0.7 305.4 %copy-start.13 = (s32[6,128]{1,0:T(8,128)S(1)}, s32[6,128]{1,0:T(8,128)}, u32[]{:S(2)}) copy-start(s32[6,128]{1,0:T(8,128)} %param.109) | copy-start | bytes 9220
  0.7 305.4 %copy-start.4 = (s32[6,128]{1,0:T(8,128)S(1)}, s32[6,128]{1,0:T(8,128)}, u32[]{:S(2)}) copy-start(s32[6,128]{1,0:T(8,128)} %param.108) | copy-start | bytes 9220
  0.7 307.3 %copy-start.2 = (f32[3,5,5,128]{3,0,2,1:T(4,128)S(1)}, f32[3,5,5,128]{3,0,2,1:T(4,128)}, u32[]{:S(2)}) copy-start(f32[3,5,5,128]{3,0,2,1:T(4,128)} %param.104) | copy-start | bytes 115204
  298.6 21.3 %collective-permute-start = (f32[5,64,32]{2,1,0:T(8,128)}, f32[5,64,32]{2,1,0:T(8,128)}, u32[]{:S(2)}, u32[]{:S(2)}) collective-permute-start(f32[5,64,32]{2,1,0:T(8,128)} %get-tuple-element.542), channel_id=1, source_target_pairs={{0,1},{1,2},{2,3},{3,4},{4,5},{5,6},{6,7},{7,8},{8,9},{9,10},{10,1... | collective-permute-start | bytes 122888 | tf_op jit(solution)/shard_map/ppermute | solution.py:15
  300.5 19.4 %collective-permute-start.1 = (f32[5,64,32]{2,1,0:T(8,128)}, f32[5,64,32]{2,1,0:T(8,128)}, u32[]{:S(2)}, u32[]{:S(2)}) collective-permute-start(f32[5,64,32]{2,1,0:T(8,128)} %get-tuple-element.543), channel_id=1, source_target_pairs={{1,0},{2,1},{3,2},{4,3},{5,4},{6,5},{7,6},{8,7},{9,8},{10,9},{11,1... | collective-permute-start | bytes 122888 | tf_op jit(solution)/shard_map/ppermute | solution.py:18
  319.8 64.1 %copy-start.11 = (f32[128]{0:T(128)}, f32[128]{0:T(128)S(1)}, u32[]{:S(2)}) copy-start(f32[128]{0:T(128)S(1)} %get-tuple-element.551) | copy-start | bytes 1540
  319.8 64.1 %copy-start.9 = (f32[128]{0:T(128)}, f32[128]{0:T(128)S(1)}, u32[]{:S(2)}) copy-start(f32[128]{0:T(128)S(1)} %get-tuple-element.550) | copy-start | bytes 1540
  319.9 64.2 %copy-start.7 = (f32[128]{0:T(128)}, f32[128]{0:T(128)S(1)}, u32[]{:S(2)}) copy-start(f32[128]{0:T(128)S(1)} %get-tuple-element.549) | copy-start | bytes 1540
  319.9 64.2 %copy-start.5 = (f32[128]{0:T(128)}, f32[128]{0:T(128)S(1)}, u32[]{:S(2)}) copy-start(f32[128]{0:T(128)S(1)} %get-tuple-element.548) | copy-start | bytes 1540
  891.3 14.3 collective-permute-start.2
  893.3 12.4 collective-permute-start.3
  965.2 4.5 copy-start.12
  965.2 4.6 copy-start.10
  965.2 4.6 copy-start.8
  965.2 4.6 copy-start.6
where the time goes:
time: 1750 us; the launch traced here: 1740 us
  blocking collectives  1520 us (87%)
  local copies, waits for them, and re-layouts  137 us (8%)
  other arithmetic  38.8 us (2%)
  between operations  18.6 us (1%)
  matrix products  17.7 us (1%)
    psum x3, blocking collectives, project_one(): return lax.psum(jnp.sum(mapped * vector), 'elem')  741 us
    psum x2, blocking collectives, orth_length(): return jnp.sqrt(lax.psum(jnp.sum(mapped * mapped), 'elem'))  496 us
    psum x1, blocking collectives, local(): start_norm = jnp.sqrt(lax.psum(jnp.sum(right_side * right_side), 'elem'))  257 us
    gather x2, local copies, waits for them, and re-layouts, operate(): jnp.take(extended.reshape(5, 64 * padded_width), flat_index, axis=1)  87.6 us
  transfers between devices with their start and end apart: 4, of which 0 were waited for; matrix products, arithmetic and copies ran while one was open for 1% of the time, Pallas kernels for 0%

commit v1 on v0

v1 whole, which is shorter than its diff:
```python
import functools

import jax
import jax.numpy as jnp
import numpy as np
from jax import lax
from jax.experimental import pallas as pl
from jax.experimental.pallas import tpu as pltpu
from jax.sharding import PartitionSpec as P

MESH = pl.DeviceIdType.MESH
F32 = jnp.float32
I32 = jnp.int32
VARS, NODES, LANES, HALO = 5, 64, 128, 32
SECTIONS, ROW, COLS = 4, 16, 8


def derivative_table():
    points = np.array([-1.0, -np.sqrt(0.2), np.sqrt(0.2), 1.0])
    weights = np.array([1.0 / np.prod([points[b] - points[c] for c in range(4) if c != b]) for b in range(4)])
    table = np.zeros((4, 4))
    for a in range(4):
        for b in range(4):
            if a != b:
                table[a, b] = weights[b] / weights[a] / (points[a] - points[b])
        table[a, a] = -np.sum(table[a])
    return table


def slope_matrix():
    table, eye = derivative_table().astype(np.float32).astype(np.float64), np.eye(4)
    parts = [np.eye(NODES)]
    for spots in ((table, eye, eye), (eye, table, eye), (eye, eye, table)):
        parts.append(np.kron(np.kron(spots[0], spots[1]), spots[2]))
    return np.concatenate(parts).astype(np.float32)


def dot(a, b):
    return jnp.dot(a, b, precision=lax.Precision.HIGHEST, preferred_element_type=F32)


def inverse_of(entries):
    left = [[entries[i][j] for j in range(4)] for i in range(4)]
    right = [[jnp.full_like(entries[0][0], 1.0 if i == j else 0.0) for j in range(4)] for i in range(4)]
    for pivot in range(4):
        scale = 1.0 / left[pivot][pivot]
        left[pivot] = [x * scale for x in left[pivot]]
        right[pivot] = [x * scale for x in right[pivot]]
        for target in range(4):
            if target != pivot:
                factor = left[target][pivot]
                left[target] = [x - factor * y for x, y in zip(left[target], left[pivot])]
                right[target] = [x - factor * y for x, y in zip(right[target], right[pivot])]
    return right


def pick(choices, which):
    out = choices[0]
    for i in range(1, len(choices)):
        out = jnp.where(which == i, choices[i], out)
    return out


def face_rows(u):
    sub = lax.broadcasted_iota(I32, (8, LANES), 0)
    low = sub < 4
    rows = [[u[0][0], u[0][1]], [u[3][0], u[3][1]], [], [], [], []]
    for h in range(2):
        a, b = u[2 * h], u[2 * h + 1]
        rows[2].append(jnp.where(low, a[0], pltpu.roll(b[0], 4, 0)))
        rows[3].append(jnp.where(low, pltpu.roll(a[1], 4, 0), b[1]))
    for f, k in ((4, 0), (5, 3)):
        at = k + 4 * (sub & 1)
        for h in range(2):
            a, b = u[2 * h], u[2 * h + 1]
            s = [jnp.take_along_axis(x, at, axis=0) for x in (a[0], a[1], b[0], b[1])]
            rows[f].append(jnp.where(low, jnp.where(sub < 2, s[0], s[1]), jnp.where(sub < 6, s[2], s[3])))
    return rows


def turned(a, b, code):
    swap = (code & 4) != 0
    a2 = jnp.where(swap, b, a)
    b2 = jnp.where(swap, a, b)
    a2 = jnp.where((code & 1) != 0, 3 - a2, a2)
    b2 = jnp.where((code & 2) != 0, 3 - b2, b2)
    return 4 * a2 + b2


def body(
    residual, transform, shifts, flux, penalty, block_inverse, nodal_inverse, neighbours, orientation, live_counts, slopes,
    out, rms,
    v_res, v_flux, v_pen, v_block, v_nodal, v_neigh, v_orient, v_slopes, s_transform, s_shift, s_live,
    n_all, mixed, blocks, pen_node, far_coef, far_row, own_at, halo_at, y, r, w, dirs, faces, near, pack, halo, red1, red2,
    in_sem, res_send, res_recv, dir_send, dir_recv, halo_send, halo_recv, red_send, red_recv,
):
    s, e = lax.axis_index("section"), lax.axis_index("elem")
    x_peers = [(lax.rem(s + k, SECTIONS), e) for k in (1, 3, 2)]
    nxt, prv = (s, lax.rem(e + 1, 128)), (s, lax.rem(e + 127, 128))
    row_base = (e // ROW) * ROW
    row_at = e - row_base
    row_peers = [(s, row_base + lax.rem(row_at + k, ROW)) for k in (8, 9, 7, 6, 10, 5, 11, 4, 12, 3, 13, 2, 14, 15, 1)]
    plane_at = s * COLS + e // ROW
    plane_peers = []
    for k in (2, 1, 3, 0):
        for q in (4, 3, 5, 2, 6, 1, 7, 0):
            if k or q:
                plane_peers.append((lax.rem(s + k, SECTIONS), lax.rem(e + ROW * q, 128)))

    barrier = pltpu.get_barrier_semaphore()
    peers = x_peers + [nxt, prv] + row_peers + plane_peers
    for p in peers:
        pl.semaphore_signal(barrier, inc=1, device_id=p, device_id_type=MESH)

    loads = [
        (residual.at[0], v_res.at[s]), (flux, v_flux), (penalty, v_pen), (block_inverse.at[0], v_block), (nodal_inverse.at[0], v_nodal),
        (neighbours, v_neigh), (orientation, v_orient), (slopes, v_slopes), (transform, s_transform), (shifts, s_shift),
        (live_counts, s_live),
    ]
    loads = [pltpu.make_async_copy(a, b, in_sem.at[i]) for i, (a, b) in enumerate(loads)]
    for c in loads:
        c.start()

    pl.semaphore_wait(barrier, len(peers))
    res_copies = []
    for j, p in enumerate(x_peers):
        c = pltpu.make_async_remote_copy(
            src_ref=residual.at[0], dst_ref=v_res.at[s], send_sem=res_send.at[j], recv_sem=res_recv.at[j], device_id=p,
            device_id_type=MESH,
        )
        c.start()
        res_copies.append(c)
    for c in loads:
        c.wait()

    lane = lax.broadcasted_iota(I32, (8, LANES), 1)
    sub = lax.broadcasted_iota(I32, (8, LANES), 0)
    mask = jnp.where(lane < s_live[0], 1.0, 0.0).astype(F32)
    mask1 = mask[0:1]
    t_entries = [[jnp.full((8, LANES), s_transform[i, j], F32) for j in range(4)] for i in range(4)]
    inverse = inverse_of(t_entries)
    mix = [pick([inverse[i][t] for i in range(4)], s) * mask for t in range(4)]
    t_row = [pick([t_entries[i][t] for i in range(4)], s) for t in range(4)]

    n_all[...] = dot(v_slopes[...], v_nodal[...])
    for m in range(VARS):
        blocks[m] = v_block[m] * mask1
    for d in range(3):
        for k in range(VARS):
            total = None
            for m in range(VARS):
                term = v_flux[d, k, m:m + 1, :] * blocks[m]
                total = term if total is None else total + term
            mixed[d, k] = total

    dead = jnp.zeros((8, LANES), F32)
    coef, code = [], []
    for f in range(6):
        far = jnp.broadcast_to(v_neigh[f:f + 1, :], (8, LANES))
        there = far >= 0
        at = far - e * LANES
        inside = there & (at >= 0) & (at < LANES)
        before = there & (at < 0)
        after = there & (at >= LANES)
        own_at[f] = jnp.where(inside, at, 0)
        halo_at[f] = jnp.where(before, at + HALO, jnp.where(after, at - LANES, 0))
        halo_at[6 + f] = jnp.where(before, 1, jnp.where(after, 2, 0))
        coef.append(jnp.where(there, jnp.broadcast_to(v_pen[f:f + 1, :], (8, LANES)), dead) * mask)
        code.append(jnp.broadcast_to(v_orient[f:f + 1, :], (8, LANES)))
    k_at, j_low = sub & 3, sub >> 2
    for n, (i, jh) in enumerate(((0, 0), (0, 1), (3, 0), (3, 1))):
        f = 0 if i == 0 else 1
        far_coef[n] = coef[f]
        far_row[n] = turned(2 * jh + j_low, k_at, code[f])
    for i in range(4):
        for jh in range(2):
            n = 4 + 2 * i + jh
            f = 2 + jh
            far_coef[n] = jnp.where(j_low == jh, coef[f], dead)
            far_row[n] = turned(jnp.full((8, LANES), i, I32), k_at, code[f])
            n += 8
            low_face = k_at < 2
            far_coef[n] = jnp.where(k_at == 0, coef[4], jnp.where(k_at == 3, coef[5], dead))
            far_row[n] = turned(jnp.full((8, LANES), i, I32), 2 * jh + j_low, jnp.where(low_face, code[4], code[5]))
    own_pen = [jnp.broadcast_to(v_pen[f:f + 1, :], (8, LANES)) for f in range(6)]
    for i in range(4):
        for jh in range(2):
            total = jnp.full((8, LANES), s_shift[0], F32)
            if i in (0, 3):
                total = total + own_pen[0 if i == 0 else 1]
            total = total + jnp.where(j_low == jh, own_pen[2 + jh], dead)
            total = total + jnp.where(k_at == 0, own_pen[4], jnp.where(k_at == 3, own_pen[5], dead))
            pen_node[2 * i + jh] = total

    for c in res_copies:
        c.wait_recv()
    for k in range(VARS):
        for q in range(8):
            rows = pl.ds(8 * q, 8)
            total = mix[0] * v_res[0, k, rows, :]
            for t in range(1, 4):
                total = total + mix[t] * v_res[t, k, rows, :]
            r[k, rows, :] = total

    dir_copies, halo_copies = [], []

    def operator(step, source, target):
        for k in range(VARS):
            y[k] = dot(n_all[...], source[k])
        for k in range(VARS):
            total = None
            for c in range(VARS):
                term = blocks[k, c:c + 1, :] * y[c, 0:NODES, :]
                total = term if total is None else total + term
            dirs[step, s, k] = total
        for k in range(VARS):
            u = [[dirs[step, s, k, pl.ds(16 * i + 8 * jh, 8), :] for jh in range(2)] for i in range(4)]
            rows = face_rows(u)
            for f in range(6):
                for h in range(2):
                    faces[f * 10 + k * 2 + h] = rows[f][h]
        group = lane >> 5
        for p in range(15):
            x = [faces[4 * p + g] for g in range(4)]
            x = [x[0]] + [pltpu.roll(x[g], 32 * g, 1) for g in range(1, 4)]
            pack[step, 0, p] = jnp.where(group < 2, jnp.where(group == 0, x[0], x[1]), jnp.where(group == 2, x[2], x[3]))
            pack[step, 1, p] = jnp.where(group < 2, jnp.where(group == 0, x[1], x[2]), jnp.where(group == 2, x[3], x[0]))
        waits = []
        for side, p in ((0, prv), (1, nxt)):
            c = pltpu.make_async_remote_copy(
                src_ref=pack.at[step, side], dst_ref=halo.at[step, side], send_sem=halo_send.at[step, side],
                recv_sem=halo_recv.at[step, side], device_id=p, device_id_type=MESH,
            )
            c.start()
            waits.append(c)
            halo_copies.append(c)
        for j, p in enumerate(x_peers):
            c = pltpu.make_async_remote_copy(
                src_ref=dirs.at[step, s], dst_ref=dirs.at[step, s], send_sem=dir_send.at[step, j],
                recv_sem=dir_recv.at[step, j], device_id=p, device_id_type=MESH,
            )
            c.start()
            dir_copies.append(c)
        for k in range(VARS):
            total = jnp.concatenate([pen_node[q] for q in range(8)], axis=0) * dirs[step, s, k]
            for d in range(3):
                for c in range(VARS):
                    total = total + mixed[d, k, c:c + 1, :] * y[c, NODES * (d + 1):NODES * (d + 2), :]
            target[k] = total
        for f in range(6):
            at = own_at[f]
            for n in range(10):
                near[f * 10 + n] = jnp.take_along_axis(faces[(f ^ 1) * 10 + n], at, axis=1)
        for c in waits:
            c.wait_recv()
        for f in range(6):
            at = halo_at[f]
            side = halo_at[6 + f]
            for n in range(10):
                m = (f ^ 1) * 10 + n
                p, g = m // 4, m % 4
                after = jnp.take_along_axis(halo[step, 0, p], at + 32 * g, axis=1)
                before = jnp.take_along_axis(halo[step, 1, p], at + 32 * ((g + 3) % 4), axis=1)
                near[f * 10 + n] = jnp.where(side == 0, near[f * 10 + n], jnp.where(side == 1, before, after))
        for n in range(20):
            row = far_row[n]
            at, high = row & 7, row >= 8
            if n < 4:
                f, i, jh = n // 2, 3 * (n // 2), n % 2
            else:
                i, jh = ((n - 4) % 8) // 2, n % 2
                f = 2 + jh if n < 12 else 4
            for k in range(VARS):
                def turn(face):
                    a = jnp.take_along_axis(near[face * 10 + 2 * k], at, axis=0)
                    b = jnp.take_along_axis(near[face * 10 + 2 * k + 1], at, axis=0)
                    return jnp.where(high, b, a)

                far = turn(f) if f < 4 else jnp.where(k_at < 2, turn(4), turn(5))
                rows = pl.ds(16 * i + 8 * jh, 8)
                target[k, rows, :] = target[k, rows, :] - far_coef[n] * far

    operator(0, r, w.at[0])
    operator(1, w.at[0], w.at[1])

    sums = [None] * 6
    for k in range(VARS):
        for q in range(8):
            rows = pl.ds(8 * q, 8)
            a, b, c = r[k, rows, :], w[0, k, rows, :], w[1, k, rows, :]
            for n, term in enumerate((a * a, a * b, b * b, a * c, b * c, c * c)):
                sums[n] = term if sums[n] is None else sums[n] + term
    stacked = dead
    for n in range(6):
        stacked = jnp.where(sub == n, jnp.sum(sums[n], axis=0, keepdims=True), stacked)
    stacked = jnp.where(sub == lane, jnp.sum(stacked, axis=1, keepdims=True), dead)
    red1[row_at] = jnp.sum(stacked, axis=0, keepdims=True)
    for p in row_peers:
        pltpu.make_async_remote_copy(
            src_ref=red1.at[row_at], dst_ref=red1.at[row_at], send_sem=red_send.at[0], recv_sem=red_recv.at[0], device_id=p,
            device_id_type=MESH,
        ).start()
    all_row = pltpu.make_async_remote_copy(
        src_ref=red1.at[pl.ds(0, ROW - 1)], dst_ref=red1.at[pl.ds(0, ROW - 1)], send_sem=red_send.at[0],
        recv_sem=red_recv.at[0], device_id=prv, device_id_type=MESH,
    )
    all_row.wait_recv()
    total = red1[0]
    for n in range(1, ROW):
        total = total + red1[n]
    red2[plane_at] = total
    for p in plane_peers:
        pltpu.make_async_remote_copy(
            src_ref=red2.at[plane_at], dst_ref=red2.at[plane_at], send_sem=red_send.at[1], recv_sem=red_recv.at[1],
            device_id=p, device_id_type=MESH,
        ).start()
    count = SECTIONS * COLS - 1
    all_plane = pltpu.make_async_remote_copy(
        src_ref=red2.at[pl.ds(0, count)], dst_ref=red2.at[pl.ds(0, count)], send_sem=red_send.at[1],
        recv_sem=red_recv.at[1], device_id=prv, device_id_type=MESH,
    )
    all_plane.wait_recv()
    one, two = [], []
    start = None
    for t in range(SECTIONS):
        total = red2[COLS * t]
        for n in range(1, COLS):
            total = total + red2[COLS * t + n]
        g = [jnp.sum(jnp.where(lane[0:1] == n, total, 0.0), axis=1, keepdims=True) for n in range(6)]
        ratio = g[4] / g[2]
        c2 = (g[3] - ratio * g[1]) / (g[5] - ratio * g[4])
        c1 = g[1] / g[2] - ratio * c2
        one.append(t_row[t] * c1)
        two.append(t_row[t] * c2)
        start = g[0] if start is None else jnp.where(s == t, g[0], start)
    rms[...] = jnp.broadcast_to(jnp.sqrt(start) / np.float32(np.sqrt(np.float32(VARS * NODES * LANES * 128))), rms.shape)
    for c in dir_copies:
        c.wait_recv()
    for k in range(VARS):
        for q in range(8):
            rows = pl.ds(8 * q, 8)
            total = None
            for t in range(SECTIONS):
                term = one[t] * dirs[0, t, k, rows, :] + two[t] * dirs[1, t, k, rows, :]
                total = term if total is None else total + term
            out[0, k, rows, :] = total
    for c in res_copies + dir_copies + halo_copies + [all_row, all_plane]:
        c.wait_send()


def local(*args):
    hbm = pl.BlockSpec(memory_space=pl.ANY)
    vmem = pl.BlockSpec(memory_space=pltpu.VMEM)
    dma = pltpu.SemaphoreType.DMA
    slopes = jnp.asarray(slope_matrix())
    update, rms = pl.pallas_call(
        body,
        out_shape=(
            jax.ShapeDtypeStruct((1, VARS, NODES, LANES), F32),
            jax.ShapeDtypeStruct((1, LANES), F32),
        ),
        in_specs=[hbm] * 11,
        out_specs=(vmem, vmem),
        scratch_shapes=[
            pltpu.VMEM((SECTIONS, VARS, NODES, LANES), F32),
            pltpu.VMEM((3, VARS, VARS, LANES), F32),
            pltpu.VMEM((6, LANES), F32),
            pltpu.VMEM((VARS, VARS, LANES), F32),
            pltpu.VMEM((NODES, NODES), F32),
            pltpu.VMEM((6, LANES), I32),
            pltpu.VMEM((6, LANES), I32),
            pltpu.VMEM((4 * NODES, NODES), F32),
            pltpu.SMEM((4, 4), F32),
            pltpu.SMEM((1,), F32),
            pltpu.SMEM((1,), I32),
            pltpu.VMEM((4 * NODES, NODES), F32),
            pltpu.VMEM((3, VARS, VARS, LANES), F32),
            pltpu.VMEM((VARS, VARS, LANES), F32),
            pltpu.VMEM((8, 8, LANES), F32),
            pltpu.VMEM((20, 8, LANES), F32),
            pltpu.VMEM((20, 8, LANES), I32),
            pltpu.VMEM((6, 8, LANES), I32),
            pltpu.VMEM((12, 8, LANES), I32),
            pltpu.VMEM((VARS, 4 * NODES, LANES), F32),
            pltpu.VMEM((VARS, NODES, LANES), F32),
            pltpu.VMEM((2, VARS, NODES, LANES), F32),
            pltpu.VMEM((2, SECTIONS, VARS, NODES, LANES), F32),
            pltpu.VMEM((60, 8, LANES), F32),
            pltpu.VMEM((60, 8, LANES), F32),
            pltpu.VMEM((2, 2, 15, 8, LANES), F32),
            pltpu.VMEM((2, 2, 15, 8, LANES), F32),
            pltpu.VMEM((ROW, 1, LANES), F32),
            pltpu.VMEM((SECTIONS * COLS, 1, LANES), F32),
            dma((11,)), dma((3,)), dma((3,)), dma((2, 3)), dma((2, 3)), dma((2, 2)), dma((2, 2)), dma((2,)), dma((2,)),
        ],
        compiler_params=pltpu.CompilerParams(collective_id=0, has_side_effects=True, vmem_limit_bytes=32 * 1024 * 1024),
        name="newton_step",
    )(*args, slopes)
    return update, rms[0, 0:1]


def solution(mesh):
    placed = (
        P("section", None, None, "elem"), P(), P("section"), P(None, None, None, "elem"), P(None, "elem"),
        P("section", None, None, "elem"), P("section", None, None), P(None, "elem"), P(None, "elem"), P("elem"),
    )
    return jax.shard_map(
        local, mesh=mesh, in_specs=placed, out_specs=(P("section", None, None, "elem"), P("section")), check_vma=False,
    )
```

time: 1750 us -> 50.9 us (0.03)
  blocking collectives: 1520 us -> 0 us
  local copies, waits for them, and re-layouts: 137 us -> 3.93 us
  Pallas kernels: 0 us -> 43.4 us
  other arithmetic: 38.8 us -> 0 us
  matrix products: 17.7 us -> 0 us
    psum x6 -> x0, blocking collectives: 1490 us -> none  [the longest x3 741 us: project_one(): return lax.psum(jnp.sum(mapped * vector), 'elem')]
    gather x2 -> x0, local copies, waits for them, and re-layouts: 87.6 us -> none  [operate(): jnp.take(extended.reshape(5, 64 * padded_width), flat_index, axis=1)]
    pallas_call x0 -> x1, Pallas kernels: none -> 43.4 us  [local(): pl.pallas_call(body, out_shape=(jax.ShapeDtypeStruct((1, VARS, NODES, LAN...]
    all_gather x2 -> x0, blocking collectives: 21.7 us -> none  [the longest x1 11.5 us: local(): lax.all_gather(section_residual, 'section', axis=0, tiled=True)]
    select_n x3 -> x0, other arithmetic: 20.7 us -> none  [the longest x2 20.7 us: operate(): jnp.take(extended.reshape(5, 64 * padded_width), flat_index, axis=1)]
    reshape x10 -> x0, local copies, waits for them, and re-layouts: 19.6 us -> none  [the longest x2 8.87 us: operate(): jnp.take(extended.reshape(5, 64 * padded_width), flat_index, axis=1)]
    dot_general x18 -> x0, matrix products: 17.7 us -> none  [the longest x6 7.49 us: operate(): jnp.einsum('kch,cfh->kfh', linear_flux_matrix[axis_direction], section_sl...]
  transfers between devices with their start and end apart: 4 -> 0, of which waited for: 0 -> 0; matrix products, arithmetic and copies ran while one was open for 1% -> 0% of each run, Pallas kernels for 0% -> 0%
where the time goes in v1:
time: 50.9 us; the launch traced here: 50.5 us
  Pallas kernels  43.4 us (85%)
  local copies, waits for them, and re-layouts  3.93 us (8%)
  between operations  3.19 us (6%)
    pallas_call x1, Pallas kernels, local(): pl.pallas_call(body, out_shape=(jax.ShapeDtypeStruct((1, VARS, NODES, LAN...  43.4 us
    unnamed x17, local copies, waits for them, and re-layouts  3.93 us

profile of v1, /device:TPU:1, one launch (start us, length us, event | category | flops | bytes accessed | tf_op | source)
XLA Modules:
  0.0 50.5 jit_solution(10945311588655871927)
XLA Ops:
  0.6 0.0 copy-start.1
  2.0 0.7 %copy.14.block_inverse = f32[1,5,5,128]{3,2,1,0:T(8,128)S(1)} copy(f32[1,5,5,128]{3,0,2,1:T(1,128)} %param.16) | data formatting | bytes 25600 | tf_op args[5]
  2.7 0.0 copy-start.3
  2.7 0.0 copy-start.4
  2.7 0.0 copy-start.5
  2.7 0.0 copy-start.6
  2.7 0.9 %copy.13.flux = f32[3,5,5,128]{3,2,1,0:T(8,128)S(1)} copy(f32[3,5,5,128]{3,0,2,1:T(4,128)} %param.14) | data formatting | bytes 76800 | tf_op args[3]
  3.6 0.0 copy-done.1
  3.6 0.0 copy-done.3
  3.6 0.0 copy-done.4
  3.6 0.0 copy-done.5
  3.6 0.0 copy-done.6
  3.6 0.0 copy-start
  3.6 0.9 %copy-done = f32[1,5,64,128]{3,2,1,0:T(8,128)S(1)} copy-done((f32[1,5,64,128]{3,2,1,0:T(8,128)S(1)}, f32[1,5,64,128]{3,2,1,0:T(8,128)}, u32[]{:S(2)}) %copy-start) | copy-done | bytes 163864
  4.5 0.0 copy-start.2
  4.5 0.8 %copy-done.2 = f32[1,64,64]{2,1,0:T(8,128)S(1)} copy-done((f32[1,64,64]{2,1,0:T(8,128)S(1)}, f32[1,64,64]{2,1,0:T(8,128)}, u32[]{:S(2)}) %copy-start.2) | copy-done | bytes 16408
  5.3 43.4 %newton_step.1 = (f32[1,5,64,128]{3,2,1,0:T(8,128)S(1)}, f32[1,128]{1,0:T(1,128)S(1)}) custom-call(f32[1,5,64,128]{3,2,1,0:T(8,128)S(1)} %copy-done, f32[4,4]{1,0:T(4,128)S(1)} %copy-done.6, f32[1]{0:T(128)S(6)} %copy.17.shifts, f32[3,5,5,128]{3,2,1,0:T(8,128)S(1)} %copy.13.flux, f32[6,128]{1,0:T(8,128)S(1)} %copy-done.3, ...), custom_call_target="tpu_custom_call" | custom-call | tf_op jit(solution)/shard_map/newton_step/pallas_call | solution.py:356
  48.7 0.7 %copy.19 = f32[1,5,64,128]{3,2,1,0:T(8,128)} copy(f32[1,5,64,128]{3,2,1,0:T(8,128)S(1)} %get-tuple-element.8) | data formatting | bytes 327680
Async XLA Ops:
  0.6 2.9 %copy-start.1 = (f32[256,64]{1,0:T(8,128)S(1)}, f32[256,64]{1,0:T(8,128)}, u32[]{:S(2)}) copy-start(f32[256,64]{1,0:T(8,128)} %constant.2.clone.slopes) | copy-start | bytes 196612
  2.7 0.9 %copy-start.3 = (f32[6,128]{1,0:T(8,128)S(1)}, f32[6,128]{1,0:T(8,128)}, u32[]{:S(2)}) copy-start(f32[6,128]{1,0:T(8,128)} %penalty.1) | copy-start | bytes 9220
  2.7 0.9 %copy-start.4 = (s32[6,128]{1,0:T(8,128)S(1)}, s32[6,128]{1,0:T(8,128)}, u32[]{:S(2)}) copy-start(s32[6,128]{1,0:T(8,128)} %neighbours.1) | copy-start | bytes 9220
  2.7 0.9 %copy-start.5 = (s32[6,128]{1,0:T(8,128)S(1)}, s32[6,128]{1,0:T(8,128)}, u32[]{:S(2)}) copy-start(s32[6,128]{1,0:T(8,128)} %orientation.1) | copy-start | bytes 9220
  2.7 0.9 %copy-start.6 = (f32[4,4]{1,0:T(4,128)S(1)}, f32[4,4]{1,0:T(4,128)}, u32[]{:S(2)}) copy-start(f32[4,4]{1,0:T(4,128)} %transform.1) | copy-start | bytes 196
  3.6 0.9 %copy-start = (f32[1,5,64,128]{3,2,1,0:T(8,128)S(1)}, f32[1,5,64,128]{3,2,1,0:T(8,128)}, u32[]{:S(2)}) copy-start(f32[1,5,64,128]{3,2,1,0:T(8,128)} %residual.1) | copy-start | bytes 491524
  4.5 0.8 %copy-start.2 = (f32[1,64,64]{2,1,0:T(8,128)S(1)}, f32[1,64,64]{2,1,0:T(8,128)}, u32[]{:S(2)}) copy-start(f32[1,64,64]{2,1,0:T(8,128)} %nodal_inverse.1) | copy-start | bytes 49156

commit v2 on v1

--- a/solution.py
+++ b/solution.py
@@ -113,7 +113,7 @@
         pl.semaphore_signal(barrier, inc=1, device_id=p, device_id_type=MESH)
 
     loads = [
-        (residual.at[0], v_res.at[s]), (flux, v_flux), (penalty, v_pen), (block_inverse.at[0], v_block), (nodal_inverse.at[0], v_nodal),
+        (residual.at[0], v_res.at[s]), (flux, v_flux), (penalty, v_pen), (block_inverse, v_block), (nodal_inverse.at[0], v_nodal),
         (neighbours, v_neigh), (orientation, v_orient), (slopes, v_slopes), (transform, s_transform), (shifts, s_shift),
         (live_counts, s_live),
     ]
@@ -144,12 +144,12 @@
 
     n_all[...] = dot(v_slopes[...], v_nodal[...])
     for m in range(VARS):
-        blocks[m] = v_block[m] * mask1
+        blocks[m] = jnp.concatenate([v_block[m, c] for c in range(VARS)], axis=0) * mask1
     for d in range(3):
         for k in range(VARS):
             total = None
             for m in range(VARS):
-                term = v_flux[d, k, m:m + 1, :] * blocks[m]
+                term = v_flux[k, m, d:d + 1, :] * blocks[m]
                 total = term if total is None else total + term
             mixed[d, k] = total
 
@@ -349,23 +349,27 @@
 
 
 def local(*args):
-    hbm = pl.BlockSpec(memory_space=pl.ANY)
+    hbm = pl.BlockSpec(memory_space=pltpu.HBM)
+    ANY = pl.BlockSpec(memory_space=pl.ANY)
     vmem = pl.BlockSpec(memory_space=pltpu.VMEM)
     dma = pltpu.SemaphoreType.DMA
     slopes = jnp.asarray(slope_matrix())
+    args = list(args)
+    args[3] = jnp.transpose(args[3], (1, 2, 0, 3))
+    args[5] = jnp.transpose(args[5], (1, 2, 0, 3))
     update, rms = pl.pallas_call(
         body,
         out_shape=(
-            jax.ShapeDtypeStruct((1, VARS, NODES, LANES), F32),
-            jax.ShapeDtypeStruct((1, LANES), F32),
+            pltpu.VMEM((1, VARS, NODES, LANES), F32),
+            pltpu.VMEM((1, LANES), F32),
         ),
-        in_specs=[hbm] * 11,
+        in_specs=[hbm, hbm, ANY] + [hbm] * 6 + [ANY, hbm],
         out_specs=(vmem, vmem),
         scratch_shapes=[
             pltpu.VMEM((SECTIONS, VARS, NODES, LANES), F32),
-            pltpu.VMEM((3, VARS, VARS, LANES), F32),
+            pltpu.VMEM((VARS, VARS, 3, LANES), F32),
             pltpu.VMEM((6, LANES), F32),
-            pltpu.VMEM((VARS, VARS, LANES), F32),
+            pltpu.VMEM((VARS, VARS, 1, LANES), F32),
             pltpu.VMEM((NODES, NODES), F32),
             pltpu.VMEM((6, LANES), I32),
             pltpu.VMEM((6, LANES), I32),
@@ -395,7 +399,7 @@
         ],
         compiler_params=pltpu.CompilerParams(collective_id=0, has_side_effects=True, vmem_limit_bytes=32 * 1024 * 1024),
         name="newton_step",
-    )(*args, slopes)
+    )(*[x if x.shape == (1,) else pltpu.with_memory_space_constraint(x, pltpu.HBM) for x in args + [slopes]])
     return update, rms[0, 0:1]
 
 

time: 50.9 us -> 47.6 us (0.935)
  local copies, waits for them, and re-layouts: 3.93 us -> 0.67 us
    unnamed x17 -> x1, local copies, waits for them, and re-layouts: 3.93 us -> 0.67 us
where the time goes in v2:
time: 47.6 us; the launch traced here: 47.4 us
  Pallas kernels  43.7 us (92%)
  between operations  3.1 us (7%)
  local copies, waits for them, and re-layouts  0.67 us (1%)
    pallas_call x1, Pallas kernels, local(): pl.pallas_call(body, out_shape=(pltpu.VMEM((1, VARS, NODES, LANES), F32),...  43.7 us

profile of v2, /device:TPU:1, one launch (start us, length us, event | category | flops | bytes accessed | tf_op | source)
XLA Modules:
  0.0 47.4 jit_solution(13292320636558526301)
XLA Ops:
  1.9 43.7 %newton_step.1 = (f32[1,5,64,128]{3,2,1,0:T(8,128)S(1)}, f32[1,128]{1,0:T(1,128)S(1)}) custom-call(f32[1,5,64,128]{3,2,1,0:T(8,128)} %residual.1, f32[4,4]{1,0:T(4,128)} %transform.1, f32[1]{0:T(128)S(6)} %copy.16.shifts, f32[5,5,3,128]{3,2,1,0:T(4,128)} %bitcast.5, f32[6,128]{1,0:T(8,128)} %penalty.1, f32[5,5,1,128]{3,2,1,0:T(1,128)} %bitcast.6, ...), custom_call_target="tpu_custom_call" | custom-call | tf_op jit(solution)/shard_map/newton_step/pallas_call | solution.py:360
  45.6 0.7 %copy.15 = f32[1,5,64,128]{3,2,1,0:T(8,128)} copy(f32[1,5,64,128]{3,2,1,0:T(8,128)S(1)} %get-tuple-element.6) | data formatting | bytes 327680

commit v3 on v2

--- a/solution.py
+++ b/solution.py
@@ -92,7 +92,7 @@
     out, rms,
     v_res, v_flux, v_pen, v_block, v_nodal, v_neigh, v_orient, v_slopes, s_transform, s_shift, s_live,
     n_all, mixed, blocks, pen_node, far_coef, far_row, own_at, halo_at, y, r, w, dirs, faces, near, pack, halo, red1, red2,
-    in_sem, res_send, res_recv, dir_send, dir_recv, halo_send, halo_recv, red_send, red_recv,
+    in_sem, res_send, res_recv, pass_send, pass_recv, dir_send, dir_recv, halo_send, halo_recv, red_send, red_recv,
 ):
     s, e = lax.axis_index("section"), lax.axis_index("elem")
     x_peers = [(lax.rem(s + k, SECTIONS), e) for k in (1, 3, 2)]
@@ -122,14 +122,18 @@
         c.start()
 
     pl.semaphore_wait(barrier, len(peers))
-    res_copies = []
-    for j, p in enumerate(x_peers):
-        c = pltpu.make_async_remote_copy(
-            src_ref=residual.at[0], dst_ref=v_res.at[s], send_sem=res_send.at[j], recv_sem=res_recv.at[j], device_id=p,
-            device_id_type=MESH,
-        )
-        c.start()
-        res_copies.append(c)
+    sides = x_peers[:2]
+    behind = [lax.rem(s + 3, SECTIONS), lax.rem(s + 1, SECTIONS)]
+    res_copies = [[None] * VARS for _ in range(2)]
+    for n in range(VARS):
+        for d in range(2):
+            k = n if d == 0 else VARS - 1 - n
+            c = pltpu.make_async_remote_copy(
+                src_ref=residual.at[0, k], dst_ref=v_res.at[s, k], send_sem=res_send.at[d, k], recv_sem=res_recv.at[d, k],
+                device_id=sides[d], device_id_type=MESH,
+            )
+            c.start()
+            res_copies[d][k] = c
     for c in loads:
         c.wait()
 
@@ -142,7 +146,18 @@
     mix = [pick([inverse[i][t] for i in range(4)], s) * mask for t in range(4)]
     t_row = [pick([t_entries[i][t] for i in range(4)], s) for t in range(4)]
 
-    n_all[...] = dot(v_slopes[...], v_nodal[...])
+    n_full = dot(v_slopes[...], v_nodal[...])
+    n_high = n_full.astype(jnp.bfloat16)
+    n_all[0:4 * NODES, :] = n_high
+    n_all[4 * NODES:8 * NODES, :] = (n_full - n_high.astype(F32)).astype(jnp.bfloat16)
+
+    def spread(k, x):
+        high = x.astype(jnp.bfloat16)
+        low = (x - high.astype(F32)).astype(jnp.bfloat16)
+        first = jnp.dot(n_all[...], high, preferred_element_type=F32)
+        second = jnp.dot(n_all[0:4 * NODES, :], low, preferred_element_type=F32)
+        y[k] = first[0:4 * NODES] + (first[4 * NODES:8 * NODES] + second)
+
     for m in range(VARS):
         blocks[m] = jnp.concatenate([v_block[m, c] for c in range(VARS)], axis=0) * mask1
     for d in range(3):
@@ -192,21 +207,40 @@
             total = total + jnp.where(k_at == 0, own_pen[4], jnp.where(k_at == 3, own_pen[5], dead))
             pen_node[2 * i + jh] = total
 
-    for c in res_copies:
-        c.wait_recv()
-    for k in range(VARS):
+    passed = [[], []]
+    for n in range(3):
+        for d in range(2):
+            k = n if d == 0 else VARS - 1 - n
+            res_copies[d][k].wait_recv()
+            rows = pl.ds(0, NODES) if n < 2 else pl.ds(NODES // 2 * d, NODES // 2)
+            part = v_res.at[behind[d], k, rows]
+            c = pltpu.make_async_remote_copy(
+                src_ref=part, dst_ref=part, send_sem=pass_send.at[d, n], recv_sem=pass_recv.at[d, n], device_id=sides[d],
+                device_id_type=MESH,
+            )
+            c.start()
+            passed[d].append(c)
+    for k in (0, 4, 1, 3, 2):
+        if k < 2:
+            res_copies[1][k].wait_recv()
+            passed[0][k].wait_recv()
+        elif k > 2:
+            res_copies[0][k].wait_recv()
+            passed[1][VARS - 1 - k].wait_recv()
+        else:
+            passed[0][2].wait_recv()
+            passed[1][2].wait_recv()
         for q in range(8):
             rows = pl.ds(8 * q, 8)
             total = mix[0] * v_res[0, k, rows, :]
             for t in range(1, 4):
                 total = total + mix[t] * v_res[t, k, rows, :]
             r[k, rows, :] = total
+        spread(k, r[k])
 
     dir_copies, halo_copies = [], []
 
-    def operator(step, source, target):
-        for k in range(VARS):
-            y[k] = dot(n_all[...], source[k])
+    def operator(step, target):
         for k in range(VARS):
             total = None
             for c in range(VARS):
@@ -280,8 +314,10 @@
                 rows = pl.ds(16 * i + 8 * jh, 8)
                 target[k, rows, :] = target[k, rows, :] - far_coef[n] * far
 
-    operator(0, r, w.at[0])
-    operator(1, w.at[0], w.at[1])
+    operator(0, w.at[0])
+    for k in range(VARS):
+        spread(k, w[0, k])
+    operator(1, w.at[1])
 
     sums = [None] * 6
     for k in range(VARS):
@@ -344,7 +380,7 @@
                 term = one[t] * dirs[0, t, k, rows, :] + two[t] * dirs[1, t, k, rows, :]
                 total = term if total is None else total + term
             out[0, k, rows, :] = total
-    for c in res_copies + dir_copies + halo_copies + [all_row, all_plane]:
+    for c in res_copies[0] + res_copies[1] + passed[0] + passed[1] + dir_copies + halo_copies + [all_row, all_plane]:
         c.wait_send()
 
 
@@ -377,7 +413,7 @@
             pltpu.SMEM((4, 4), F32),
             pltpu.SMEM((1,), F32),
             pltpu.SMEM((1,), I32),
-            pltpu.VMEM((4 * NODES, NODES), F32),
+            pltpu.VMEM((8 * NODES, NODES), jnp.bfloat16),
             pltpu.VMEM((3, VARS, VARS, LANES), F32),
             pltpu.VMEM((VARS, VARS, LANES), F32),
             pltpu.VMEM((8, 8, LANES), F32),
@@ -395,7 +431,7 @@
             pltpu.VMEM((2, 2, 15, 8, LANES), F32),
             pltpu.VMEM((ROW, 1, LANES), F32),
             pltpu.VMEM((SECTIONS * COLS, 1, LANES), F32),
-            dma((11,)), dma((3,)), dma((3,)), dma((2, 3)), dma((2, 3)), dma((2, 2)), dma((2, 2)), dma((2,)), dma((2,)),
+            dma((11,)), dma((2, VARS)), dma((2, VARS)), dma((2, 3)), dma((2, 3)), dma((2, 3)), dma((2, 3)), dma((2, 2)), dma((2, 2)), dma((2,)), dma((2,)),
         ],
         compiler_params=pltpu.CompilerParams(collective_id=0, has_side_effects=True, vmem_limit_bytes=32 * 1024 * 1024),
         name="newton_step",

time: 47.6 us -> 46.1 us (0.968)
  Pallas kernels: 43.7 us -> 42.2 us
    pallas_call x1, Pallas kernels: 43.7 us -> 42.2 us  [local(): pl.pallas_call(body, out_shape=(pltpu.VMEM((1, VARS, NODES, LANES), F32),...]
where the time goes in v3:
time: 46.1 us; the launch traced here: 45.9 us
  Pallas kernels  42.2 us (92%)
  between operations  3.1 us (7%)
  local copies, waits for them, and re-layouts  0.67 us (1%)
    pallas_call x1, Pallas kernels, local(): pl.pallas_call(body, out_shape=(pltpu.VMEM((1, VARS, NODES, LANES), F32),...  42.2 us

profile of v3, /device:TPU:1, one launch (start us, length us, event | category | flops | bytes accessed | tf_op | source)
XLA Modules:
  0.0 45.9 jit_solution(10972808542395986034)
XLA Ops:
  1.9 42.2 %newton_step.1 = (f32[1,5,64,128]{3,2,1,0:T(8,128)S(1)}, f32[1,128]{1,0:T(1,128)S(1)}) custom-call(f32[1,5,64,128]{3,2,1,0:T(8,128)} %residual.1, f32[4,4]{1,0:T(4,128)} %transform.1, f32[1]{0:T(128)S(6)} %copy.16.shifts, f32[5,5,3,128]{3,2,1,0:T(4,128)} %bitcast.5, f32[6,128]{1,0:T(8,128)} %penalty.1, f32[5,5,1,128]{3,2,1,0:T(1,128)} %bitcast.6, ...), custom_call_target="tpu_custom_call" | custom-call | tf_op jit(solution)/shard_map/newton_step/pallas_call | solution.py:396
  44.1 0.7 %copy.15 = f32[1,5,64,128]{3,2,1,0:T(8,128)} copy(f32[1,5,64,128]{3,2,1,0:T(8,128)S(1)} %get-tuple-element.6) | data formatting | bytes 327680

commit v4 on v3

--- a/solution.py
+++ b/solution.py
@@ -92,7 +92,7 @@
     out, rms,
     v_res, v_flux, v_pen, v_block, v_nodal, v_neigh, v_orient, v_slopes, s_transform, s_shift, s_live,
     n_all, mixed, blocks, pen_node, far_coef, far_row, own_at, halo_at, y, r, w, dirs, faces, near, pack, halo, red1, red2,
-    in_sem, res_send, res_recv, pass_send, pass_recv, dir_send, dir_recv, halo_send, halo_recv, red_send, red_recv,
+    in_sem, res_send, res_recv, pass_send, pass_recv, dir_send, dir_recv, across_send, across_recv, halo_send, halo_recv, red_send, red_recv,
 ):
     s, e = lax.axis_index("section"), lax.axis_index("elem")
     x_peers = [(lax.rem(s + k, SECTIONS), e) for k in (1, 3, 2)]
@@ -238,7 +238,18 @@
             r[k, rows, :] = total
         spread(k, r[k])
 
-    dir_copies, halo_copies = [], []
+    dir_copies, across_copies, halo_copies = [], [], []
+
+    def pass_on(step):
+        for d in range(2):
+            dir_copies[2 * step + d].wait_recv()
+            part = dirs.at[step, behind[d], pl.ds(0, VARS), pl.ds(NODES // 2 * d, NODES // 2)]
+            c = pltpu.make_async_remote_copy(
+                src_ref=part, dst_ref=part, send_sem=across_send.at[step, d], recv_sem=across_recv.at[step, d],
+                device_id=sides[d], device_id_type=MESH,
+            )
+            c.start()
+            across_copies.append(c)
 
     def operator(step, target):
         for k in range(VARS):
@@ -268,13 +279,15 @@
             c.start()
             waits.append(c)
             halo_copies.append(c)
-        for j, p in enumerate(x_peers):
+        for d in range(2):
             c = pltpu.make_async_remote_copy(
-                src_ref=dirs.at[step, s], dst_ref=dirs.at[step, s], send_sem=dir_send.at[step, j],
-                recv_sem=dir_recv.at[step, j], device_id=p, device_id_type=MESH,
+                src_ref=dirs.at[step, s], dst_ref=dirs.at[step, s], send_sem=dir_send.at[step, d],
+                recv_sem=dir_recv.at[step, d], device_id=sides[d], device_id_type=MESH,
             )
             c.start()
             dir_copies.append(c)
+        if step == 1:
+            pass_on(0)
         for k in range(VARS):
             total = jnp.concatenate([pen_node[q] for q in range(8)], axis=0) * dirs[step, s, k]
             for d in range(3):
@@ -340,6 +353,7 @@
         src_ref=red1.at[pl.ds(0, ROW - 1)], dst_ref=red1.at[pl.ds(0, ROW - 1)], send_sem=red_send.at[0],
         recv_sem=red_recv.at[0], device_id=prv, device_id_type=MESH,
     )
+    pass_on(1)
     all_row.wait_recv()
     total = red1[0]
     for n in range(1, ROW):
@@ -370,7 +384,7 @@
         two.append(t_row[t] * c2)
         start = g[0] if start is None else jnp.where(s == t, g[0], start)
     rms[...] = jnp.broadcast_to(jnp.sqrt(start) / np.float32(np.sqrt(np.float32(VARS * NODES * LANES * 128))), rms.shape)
-    for c in dir_copies:
+    for c in across_copies:
         c.wait_recv()
     for k in range(VARS):
         for q in range(8):
@@ -380,7 +394,7 @@
                 term = one[t] * dirs[0, t, k, rows, :] + two[t] * dirs[1, t, k, rows, :]
                 total = term if total is None else total + term
             out[0, k, rows, :] = total
-    for c in res_copies[0] + res_copies[1] + passed[0] + passed[1] + dir_copies + halo_copies + [all_row, all_plane]:
+    for c in res_copies[0] + res_copies[1] + passed[0] + passed[1] + dir_copies + across_copies + halo_copies + [all_row, all_plane]:
         c.wait_send()
 
 
@@ -431,7 +445,8 @@
             pltpu.VMEM((2, 2, 15, 8, LANES), F32),
             pltpu.VMEM((ROW, 1, LANES), F32),
             pltpu.VMEM((SECTIONS * COLS, 1, LANES), F32),
-            dma((11,)), dma((2, VARS)), dma((2, VARS)), dma((2, 3)), dma((2, 3)), dma((2, 3)), dma((2, 3)), dma((2, 2)), dma((2, 2)), dma((2,)), dma((2,)),
+            dma((11,)), dma((2, VARS)), dma((2, VARS)), dma((2, 3)), dma((2, 3)), dma((2, 2)), dma((2, 2)), dma((2, 2)), dma((2, 2)),
+            dma((2, 2)), dma((2, 2)), dma((2,)), dma((2,)),
         ],
         compiler_params=pltpu.CompilerParams(collective_id=0, has_side_effects=True, vmem_limit_bytes=32 * 1024 * 1024),
         name="newton_step",

time: 46.1 us -> 46.1 us (level)
  no operation moved by 1% of the time
where the time goes in v4:
time: 46.1 us; the launch traced here: 46 us
  Pallas kernels  42.2 us (92%)
  between operations  3.1 us (7%)
  local copies, waits for them, and re-layouts  0.67 us (1%)
    pallas_call x1, Pallas kernels, local(): pl.pallas_call(body, out_shape=(pltpu.VMEM((1, VARS, NODES, LANES), F32),...  42.2 us

profile of v4, /device:TPU:1, one launch (start us, length us, event | category | flops | bytes accessed | tf_op | source)
XLA Modules:
  0.0 46.0 jit_solution(15528019555972275553)
XLA Ops:
  1.9 42.2 %newton_step.1 = (f32[1,5,64,128]{3,2,1,0:T(8,128)S(1)}, f32[1,128]{1,0:T(1,128)S(1)}) custom-call(f32[1,5,64,128]{3,2,1,0:T(8,128)} %residual.1, f32[4,4]{1,0:T(4,128)} %transform.1, f32[1]{0:T(128)S(6)} %copy.16.shifts, f32[5,5,3,128]{3,2,1,0:T(4,128)} %bitcast.5, f32[6,128]{1,0:T(8,128)} %penalty.1, f32[5,5,1,128]{3,2,1,0:T(1,128)} %bitcast.6, ...), custom_call_target="tpu_custom_call" | custom-call | tf_op jit(solution)/shard_map/newton_step/pallas_call | solution.py:410
  44.1 0.7 %copy.15 = f32[1,5,64,128]{3,2,1,0:T(8,128)} copy(f32[1,5,64,128]{3,2,1,0:T(8,128)S(1)} %get-tuple-element.6) | data formatting | bytes 327680

commit v5 on v4

--- a/solution.py
+++ b/solution.py
@@ -92,7 +92,7 @@
     out, rms,
     v_res, v_flux, v_pen, v_block, v_nodal, v_neigh, v_orient, v_slopes, s_transform, s_shift, s_live,
     n_all, mixed, blocks, pen_node, far_coef, far_row, own_at, halo_at, y, r, w, dirs, faces, near, pack, halo, red1, red2,
-    in_sem, res_send, res_recv, pass_send, pass_recv, dir_send, dir_recv, across_send, across_recv, halo_send, halo_recv, red_send, red_recv,
+    in_sem, res_send, res_recv, pass_send, pass_recv, dir_send, dir_recv, across_send, across_recv, halo_send, halo_recv, red_send, red_recv, near_sem,
 ):
     s, e = lax.axis_index("section"), lax.axis_index("elem")
     x_peers = [(lax.rem(s + k, SECTIONS), e) for k in (1, 3, 2)]
@@ -108,9 +108,24 @@
                 plane_peers.append((lax.rem(s + k, SECTIONS), lax.rem(e + ROW * q, 128)))
 
     barrier = pltpu.get_barrier_semaphore()
-    peers = x_peers + [nxt, prv] + row_peers + plane_peers
+    def along_row(k):
+        return [(s, row_base + lax.rem(row_at + 2 * q, ROW)) for q in (k, COLS - k)]
+
+    def along_column(k):
+        return [(s, lax.rem(e + ROW * q, 128)) for q in (k, COLS - k)]
+
+    peers = x_peers[:2] + [nxt, prv] + along_row(1) + along_column(1)
     for p in peers:
         pl.semaphore_signal(barrier, inc=1, device_id=p, device_id_type=MESH)
+    rounds = [along_row(1), along_row(2), along_row(1), along_column(1), along_column(2), along_column(1)]
+
+    def tell(n):
+        for p in rounds[n]:
+            pl.semaphore_signal(near_sem.at[n], inc=1, device_id=p, device_id_type=MESH)
+
+    def hear(n):
+        pl.semaphore_wait(near_sem.at[n], 2)
+
 
     loads = [
         (residual.at[0], v_res.at[s]), (flux, v_flux), (penalty, v_pen), (block_inverse, v_block), (nodal_inverse.at[0], v_nodal),
@@ -134,6 +149,7 @@
             )
             c.start()
             res_copies[d][k] = c
+    tell(0)
     for c in loads:
         c.wait()
 
@@ -168,6 +184,8 @@
                 total = term if total is None else total + term
             mixed[d, k] = total
 
+    hear(0)
+    tell(1)
     dead = jnp.zeros((8, LANES), F32)
     coef, code = [], []
     for f in range(6):
@@ -207,6 +225,8 @@
             total = total + jnp.where(k_at == 0, own_pen[4], jnp.where(k_at == 3, own_pen[5], dead))
             pen_node[2 * i + jh] = total
 
+    hear(1)
+    tell(2)
     passed = [[], []]
     for n in range(3):
         for d in range(2):
@@ -220,6 +240,8 @@
             )
             c.start()
             passed[d].append(c)
+    hear(2)
+    tell(3)
     for k in (0, 4, 1, 3, 2):
         if k < 2:
             res_copies[1][k].wait_recv()
@@ -298,6 +320,8 @@
             at = own_at[f]
             for n in range(10):
                 near[f * 10 + n] = jnp.take_along_axis(faces[(f ^ 1) * 10 + n], at, axis=1)
+        hear(3 + step)
+        tell(4 + step)
         for c in waits:
             c.wait_recv()
         for f in range(6):
@@ -343,6 +367,7 @@
     for n in range(6):
         stacked = jnp.where(sub == n, jnp.sum(sums[n], axis=0, keepdims=True), stacked)
     stacked = jnp.where(sub == lane, jnp.sum(stacked, axis=1, keepdims=True), dead)
+    hear(5)
     red1[row_at] = jnp.sum(stacked, axis=0, keepdims=True)
     for p in row_peers:
         pltpu.make_async_remote_copy(
@@ -446,7 +471,7 @@
             pltpu.VMEM((ROW, 1, LANES), F32),
             pltpu.VMEM((SECTIONS * COLS, 1, LANES), F32),
             dma((11,)), dma((2, VARS)), dma((2, VARS)), dma((2, 3)), dma((2, 3)), dma((2, 2)), dma((2, 2)), dma((2, 2)), dma((2, 2)),
-            dma((2, 2)), dma((2, 2)), dma((2,)), dma((2,)),
+            dma((2, 2)), dma((2, 2)), dma((2,)), dma((2,)), pltpu.SemaphoreType.REGULAR((6,)),
         ],
         compiler_params=pltpu.CompilerParams(collective_id=0, has_side_effects=True, vmem_limit_bytes=32 * 1024 * 1024),
         name="newton_step",

time: 46.1 us -> 44.9 us (0.974)
  Pallas kernels: 42.2 us -> 41 us
    pallas_call x1, Pallas kernels: 42.2 us -> 41 us  [local(): pl.pallas_call(body, out_shape=(pltpu.VMEM((1, VARS, NODES, LANES), F32),...]
where the time goes in v5:
time: 44.9 us; the launch traced here: 44.8 us
  Pallas kernels  41 us (91%)
  between operations  3.1 us (7%)
  local copies, waits for them, and re-layouts  0.67 us (1%)
    pallas_call x1, Pallas kernels, local(): pl.pallas_call(body, out_shape=(pltpu.VMEM((1, VARS, NODES, LANES), F32),...  41 us

profile of v5, /device:TPU:1, one launch (start us, length us, event | category | flops | bytes accessed | tf_op | source)
XLA Modules:
  0.0 44.8 jit_solution(3357973838640046124)
XLA Ops:
  1.9 41.0 %newton_step.1 = (f32[1,5,64,128]{3,2,1,0:T(8,128)S(1)}, f32[1,128]{1,0:T(1,128)S(1)}) custom-call(f32[1,5,64,128]{3,2,1,0:T(8,128)} %residual.1, f32[4,4]{1,0:T(4,128)} %transform.1, f32[1]{0:T(128)S(6)} %copy.16.shifts, f32[5,5,3,128]{3,2,1,0:T(4,128)} %bitcast.5, f32[6,128]{1,0:T(8,128)} %penalty.1, f32[5,5,1,128]{3,2,1,0:T(1,128)} %bitcast.6, ...), custom_call_target="tpu_custom_call" | custom-call | tf_op jit(solution)/shard_map/newton_step/pallas_call | solution.py:435
  42.9 0.7 %copy.15 = f32[1,5,64,128]{3,2,1,0:T(8,128)} copy(f32[1,5,64,128]{3,2,1,0:T(8,128)S(1)} %get-tuple-element.6) | data formatting | bytes 327680

commit v6 on v5

--- a/solution.py
+++ b/solution.py
@@ -159,8 +159,11 @@
     mask1 = mask[0:1]
     t_entries = [[jnp.full((8, LANES), s_transform[i, j], F32) for j in range(4)] for i in range(4)]
     inverse = inverse_of(t_entries)
-    mix = [pick([inverse[i][t] for i in range(4)], s) * mask for t in range(4)]
-    t_row = [pick([t_entries[i][t] for i in range(4)], s) for t in range(4)]
+    size = [jnp.maximum(sum(jnp.abs(x) for x in row), 1.0) for row in inverse]
+    own_size = pick(size, s)
+    scale = mask / own_size
+    mix = [pick([inverse[i][t] for i in range(4)], s) * scale for t in range(4)]
+    t_row = [pick([t_entries[i][t] for i in range(4)], s) * size[t] for t in range(4)]
 
     n_full = dot(v_slopes[...], v_nodal[...])
     n_high = n_full.astype(jnp.bfloat16)
@@ -186,6 +189,21 @@
 
     hear(0)
     tell(1)
+    passed = [[], []]
+    for n in range(3):
+        for d in range(2):
+            k = n if d == 0 else VARS - 1 - n
+            res_copies[d][k].wait_recv()
+            rows = pl.ds(0, NODES) if n < 2 else pl.ds(NODES // 2 * d, NODES // 2)
+            part = v_res.at[behind[d], k, rows]
+            c = pltpu.make_async_remote_copy(
+                src_ref=part, dst_ref=part, send_sem=pass_send.at[d, n], recv_sem=pass_recv.at[d, n], device_id=sides[d],
+                device_id_type=MESH,
+            )
+            c.start()
+            passed[d].append(c)
+    hear(1)
+    tell(2)
     dead = jnp.zeros((8, LANES), F32)
     coef, code = [], []
     for f in range(6):
@@ -225,21 +243,6 @@
             total = total + jnp.where(k_at == 0, own_pen[4], jnp.where(k_at == 3, own_pen[5], dead))
             pen_node[2 * i + jh] = total
 
-    hear(1)
-    tell(2)
-    passed = [[], []]
-    for n in range(3):
-        for d in range(2):
-            k = n if d == 0 else VARS - 1 - n
-            res_copies[d][k].wait_recv()
-            rows = pl.ds(0, NODES) if n < 2 else pl.ds(NODES // 2 * d, NODES // 2)
-            part = v_res.at[behind[d], k, rows]
-            c = pltpu.make_async_remote_copy(
-                src_ref=part, dst_ref=part, send_sem=pass_send.at[d, n], recv_sem=pass_recv.at[d, n], device_id=sides[d],
-                device_id_type=MESH,
-            )
-            c.start()
-            passed[d].append(c)
     hear(2)
     tell(3)
     for k in (0, 4, 1, 3, 2):
@@ -395,20 +398,21 @@
         recv_sem=red_recv.at[1], device_id=prv, device_id_type=MESH,
     )
     all_plane.wait_recv()
-    one, two = [], []
-    start = None
+    totals = []
     for t in range(SECTIONS):
         total = red2[COLS * t]
         for n in range(1, COLS):
             total = total + red2[COLS * t + n]
-        g = [jnp.sum(jnp.where(lane[0:1] == n, total, 0.0), axis=1, keepdims=True) for n in range(6)]
-        ratio = g[4] / g[2]
-        c2 = (g[3] - ratio * g[1]) / (g[5] - ratio * g[4])
-        c1 = g[1] / g[2] - ratio * c2
-        one.append(t_row[t] * c1)
-        two.append(t_row[t] * c2)
-        start = g[0] if start is None else jnp.where(s == t, g[0], start)
-    rms[...] = jnp.broadcast_to(jnp.sqrt(start) / np.float32(np.sqrt(np.float32(VARS * NODES * LANES * 128))), rms.shape)
+        totals.append(total)
+    totals = jnp.concatenate(totals, axis=0)
+    g = [jnp.sum(jnp.where(lane[0:SECTIONS] == n, totals, 0.0), axis=1, keepdims=True) for n in range(6)]
+    ratio = g[4] / g[2]
+    c2 = (g[3] - ratio * g[1]) / (g[5] - ratio * g[4])
+    c1 = g[1] / g[2] - ratio * c2
+    one = [t_row[t] * c1[t:t + 1] for t in range(SECTIONS)]
+    two = [t_row[t] * c2[t:t + 1] for t in range(SECTIONS)]
+    start = jnp.sum(jnp.where(lax.broadcasted_iota(I32, (SECTIONS, 1), 0) == s, g[0], 0.0), axis=0, keepdims=True)
+    rms[...] = own_size[0:1] * (jnp.sqrt(start) / np.float32(np.sqrt(np.float32(VARS * NODES * LANES * 128))))
     for c in across_copies:
         c.wait_recv()
     for k in range(VARS):

time: 44.9 us -> 44.9 us (level)
  no operation moved by 1% of the time
where the time goes in v6:
time: 44.9 us; the launch traced here: 44.7 us
  Pallas kernels  41 us (91%)
  between operations  3.1 us (7%)
  local copies, waits for them, and re-layouts  0.67 us (1%)
    pallas_call x1, Pallas kernels, local(): pl.pallas_call(body, out_shape=(pltpu.VMEM((1, VARS, NODES, LANES), F32),...  41 us

profile of v6, /device:TPU:1, one launch (start us, length us, event | category | flops | bytes accessed | tf_op | source)
XLA Modules:
  0.0 44.7 jit_solution(8804539069205501729)
XLA Ops:
  1.9 41.0 %newton_step.1 = (f32[1,5,64,128]{3,2,1,0:T(8,128)S(1)}, f32[1,128]{1,0:T(1,128)S(1)}) custom-call(f32[1,5,64,128]{3,2,1,0:T(8,128)} %residual.1, f32[4,4]{1,0:T(4,128)} %transform.1, f32[1]{0:T(128)S(6)} %copy.16.shifts, f32[5,5,3,128]{3,2,1,0:T(4,128)} %bitcast.5, f32[6,128]{1,0:T(8,128)} %penalty.1, f32[5,5,1,128]{3,2,1,0:T(1,128)} %bitcast.6, ...), custom_call_target="tpu_custom_call" | custom-call | tf_op jit(solution)/shard_map/newton_step/pallas_call | solution.py:439
  42.9 0.7 %copy.15 = f32[1,5,64,128]{3,2,1,0:T(8,128)} copy(f32[1,5,64,128]{3,2,1,0:T(8,128)S(1)} %get-tuple-element.6) | data formatting | bytes 327680

commit v7 on v6

--- a/solution.py
+++ b/solution.py
@@ -276,6 +276,21 @@
             c.start()
             across_copies.append(c)
 
+    sums = []
+
+    def add_products(pairs):
+        here = [None] * len(pairs)
+        for k in range(VARS):
+            for q in range(8):
+                rows = pl.ds(8 * q, 8)
+                v = {}
+                for n in sorted({m for pair in pairs for m in pair}):
+                    v[n] = r[k, rows, :] if n == 0 else w[n - 1, k, rows, :]
+                for n, (i, j) in enumerate(pairs):
+                    term = v[i] * v[j]
+                    here[n] = term if here[n] is None else here[n] + term
+        sums.extend(here)
+
     def operator(step, target):
         for k in range(VARS):
             total = None
@@ -296,7 +311,8 @@
             pack[step, 0, p] = jnp.where(group < 2, jnp.where(group == 0, x[0], x[1]), jnp.where(group == 2, x[2], x[3]))
             pack[step, 1, p] = jnp.where(group < 2, jnp.where(group == 0, x[1], x[2]), jnp.where(group == 2, x[3], x[0]))
         waits = []
-        for side, p in ((0, prv), (1, nxt)):
+        odd = lax.rem(e, 2)
+        for side, p in ((odd, (s, lax.rem(e + 127 + 2 * odd, 128))), (1 - odd, (s, lax.rem(e + 1 + 126 * odd, 128)))):
             c = pltpu.make_async_remote_copy(
                 src_ref=pack.at[step, side], dst_ref=halo.at[step, side], send_sem=halo_send.at[step, side],
                 recv_sem=halo_recv.at[step, side], device_id=p, device_id_type=MESH,
@@ -323,6 +339,8 @@
             at = own_at[f]
             for n in range(10):
                 near[f * 10 + n] = jnp.take_along_axis(faces[(f ^ 1) * 10 + n], at, axis=1)
+        if step == 1:
+            add_products(((0, 0), (0, 1), (1, 1)))
         hear(3 + step)
         tell(4 + step)
         for c in waits:
@@ -359,13 +377,7 @@
         spread(k, w[0, k])
     operator(1, w.at[1])
 
-    sums = [None] * 6
-    for k in range(VARS):
-        for q in range(8):
-            rows = pl.ds(8 * q, 8)
-            a, b, c = r[k, rows, :], w[0, k, rows, :], w[1, k, rows, :]
-            for n, term in enumerate((a * a, a * b, b * b, a * c, b * c, c * c)):
-                sums[n] = term if sums[n] is None else sums[n] + term
+    add_products(((0, 2), (1, 2), (2, 2)))
     stacked = dead
     for n in range(6):
         stacked = jnp.where(sub == n, jnp.sum(sums[n], axis=0, keepdims=True), stacked)

time: 44.9 us -> 44.9 us (level)
  no operation moved by 1% of the time
where the time goes in v7:
time: 44.9 us; the launch traced here: 44.7 us
  Pallas kernels  41 us (91%)
  between operations  3.1 us (7%)
  local copies, waits for them, and re-layouts  0.67 us (1%)
    pallas_call x1, Pallas kernels, local(): pl.pallas_call(body, out_shape=(pltpu.VMEM((1, VARS, NODES, LANES), F32),...  41 us

profile of v7, /device:TPU:1, one launch (start us, length us, event | category | flops | bytes accessed | tf_op | source)
XLA Modules:
  0.0 44.7 jit_solution(13386168159135624150)
XLA Ops:
  1.9 41.0 %newton_step.1 = (f32[1,5,64,128]{3,2,1,0:T(8,128)S(1)}, f32[1,128]{1,0:T(1,128)S(1)}) custom-call(f32[1,5,64,128]{3,2,1,0:T(8,128)} %residual.1, f32[4,4]{1,0:T(4,128)} %transform.1, f32[1]{0:T(128)S(6)} %copy.16.shifts, f32[5,5,3,128]{3,2,1,0:T(4,128)} %bitcast.5, f32[6,128]{1,0:T(8,128)} %penalty.1, f32[5,5,1,128]{3,2,1,0:T(1,128)} %bitcast.6, ...), custom_call_target="tpu_custom_call" | custom-call | tf_op jit(solution)/shard_map/newton_step/pallas_call | solution.py:451
  42.9 0.7 %copy.15 = f32[1,5,64,128]{3,2,1,0:T(8,128)} copy(f32[1,5,64,128]{3,2,1,0:T(8,128)S(1)} %get-tuple-element.6) | data formatting | bytes 327680

commit v8 on v7

--- a/solution.py
+++ b/solution.py
@@ -311,8 +311,7 @@
             pack[step, 0, p] = jnp.where(group < 2, jnp.where(group == 0, x[0], x[1]), jnp.where(group == 2, x[2], x[3]))
             pack[step, 1, p] = jnp.where(group < 2, jnp.where(group == 0, x[1], x[2]), jnp.where(group == 2, x[3], x[0]))
         waits = []
-        odd = lax.rem(e, 2)
-        for side, p in ((odd, (s, lax.rem(e + 127 + 2 * odd, 128))), (1 - odd, (s, lax.rem(e + 1 + 126 * odd, 128)))):
+        for side, p in ((0, prv), (1, nxt)):
             c = pltpu.make_async_remote_copy(
                 src_ref=pack.at[step, side], dst_ref=halo.at[step, side], send_sem=halo_send.at[step, side],
                 recv_sem=halo_recv.at[step, side], device_id=p, device_id_type=MESH,

time: 44.9 us -> 44.9 us (level)
  no operation moved by 1% of the time
where the time goes in v8:
time: 44.9 us; the launch traced here: 44.7 us
  Pallas kernels  41 us (91%)
  between operations  3.1 us (7%)
  local copies, waits for them, and re-layouts  0.67 us (1%)
    pallas_call x1, Pallas kernels, local(): pl.pallas_call(body, out_shape=(pltpu.VMEM((1, VARS, NODES, LANES), F32),...  41 us

profile of v8, /device:TPU:1, one launch (start us, length us, event | category | flops | bytes accessed | tf_op | source)
XLA Modules:
  0.0 44.7 jit_solution(5061484091157207225)
XLA Ops:
  1.9 41.0 %newton_step.1 = (f32[1,5,64,128]{3,2,1,0:T(8,128)S(1)}, f32[1,128]{1,0:T(1,128)S(1)}) custom-call(f32[1,5,64,128]{3,2,1,0:T(8,128)} %residual.1, f32[4,4]{1,0:T(4,128)} %transform.1, f32[1]{0:T(128)S(6)} %copy.16.shifts, f32[5,5,3,128]{3,2,1,0:T(4,128)} %bitcast.5, f32[6,128]{1,0:T(8,128)} %penalty.1, f32[5,5,1,128]{3,2,1,0:T(1,128)} %bitcast.6, ...), custom_call_target="tpu_custom_call" | custom-call | tf_op jit(solution)/shard_map/newton_step/pallas_call | solution.py:450
  42.9 0.7 %copy.15 = f32[1,5,64,128]{3,2,1,0:T(8,128)} copy(f32[1,5,64,128]{3,2,1,0:T(8,128)S(1)} %get-tuple-element.6) | data formatting | bytes 327680
